TPU v7x, 128 devices: a whole 4x4x4 slice. The times are simulated.
128 devices in a mesh: space: 16 (over y_lo, z, core), set: 8 (over y_hi, x).
Axes of the slice: x: 4, y: 4 (y_hi: 2, y_lo: 2; y = y_hi * 2 + y_lo), z: 4, core: 2. Of those that a mesh axis runs over, the one named last changes fastest.
Arguments:
- initial: float32 [16, 128, 256, 128], P('set', 'space'), may hold values from -6 to 6
- conductivity: float32 [128, 256, 128], P('space'), may hold values from 0.3 to 1
- weights: float32 [16, 128, 256, 128], P('set', 'space'), may hold values from -6 to 6
- setting_index: int32 [16], P('set'), may hold values from 0 to 63
- track: int32 [64, 4], replicated, may hold values from 0 to 255
- power: int32 [64, 4], replicated, may hold values from 0 to 3
Outputs:
- final_temperature: float32 [16, 128, 256, 128], P('set', 'space')
- conductivity_gradient: float32 [128, 256, 128], P('space', 'set')
All inputs are finite; a program needn't handle non-finite values.
Results may differ from a plain program's by a relative error of at most 0.00002.
Values sent between devices are 32-bit elements; how exact they have to be, the bound alone decides.
A program may use at most 128 MiB of HBM per device.

v0:
```python
import jax
import jax.numpy as jnp
from jax import lax
from jax.sharding import PartitionSpec as P

STEPS = 4


DT = 0.15


def with_halo(shard, sides, width):
    for axis, dim in sides:
        size, length = (lax.axis_size(axis), shard.shape[dim])
        up = [(i, (i + 1) % size) for i in range(size - 1)]
        down = [(j, i) for i, j in up]
        last = lax.slice_in_dim(shard, length - width, length, axis=dim)
        initial = lax.slice_in_dim(shard, 0, width, axis=dim)
        before = lax.ppermute(last, axis, up)
        after = lax.ppermute(initial, axis, down)
        shard = jnp.concatenate([before, shard, after], axis=dim)
    return shard


def conduct(thermal):
    return 1.0 / (1.0 + thermal * thermal)


def conduct_slope(thermal):
    inverse = 1.0 / (1.0 + thermal * thermal)
    return -2.0 * thermal * inverse * inverse


def pad_cross(values):
    return jnp.pad(values, ((0, 0), (0, 0), (1, 1), (1, 1)))


def neighbours(padded):
    return [
        padded[:, 2:, 1:-1, 1:-1],
        padded[:, :-2, 1:-1, 1:-1],
        padded[:, 1:-1, 2:, 1:-1],
        padded[:, 1:-1, :-2, 1:-1],
        padded[:, 1:-1, 1:-1, 2:],
        padded[:, 1:-1, 1:-1, :-2],
    ]


def local(initial, conductivity, weights, setting_index, track, power):
    y_count = initial.shape[2]
    z_count = initial.shape[3]
    onehot = (
        setting_index[:, None] == jnp.arange(track.shape[0], dtype=jnp.int32)[None, :]
    ).astype(jnp.int32)
    y_track = jnp.sum(onehot[:, :, None] * track[None], axis=1)
    levels = jnp.sum(onehot[:, :, None] * power[None], axis=1)
    y_cells = jnp.arange(y_count).astype(jnp.float32)
    z_cells = jnp.arange(z_count).astype(jnp.float32)
    prof_z = jnp.exp(-4.0 * z_cells / z_count)
    kappa = conductivity[None]
    saved = []
    thermal = initial
    for index_step in range(STEPS):
        coeffs = kappa * conduct(thermal)
        stacked = with_halo(jnp.stack((thermal, coeffs)), (("space", 2),), 1)
        temp_ext = stacked[0]
        coef_ext = stacked[1]
        padded_temp = pad_cross(temp_ext)
        padded_coef = pad_cross(coef_ext)
        saved.append((padded_temp, padded_coef))
        centre_coef = padded_coef[:, 1:-1, 1:-1, 1:-1]
        flux = jnp.zeros_like(thermal)
        for near_temp, near_coef in zip(neighbours(padded_temp), neighbours(padded_coef)):
            flux = flux + 0.5 * (centre_coef + near_coef) * (near_temp - thermal)
        y_start = y_track[:, index_step].astype(jnp.float32)
        power_level = levels[:, index_step].astype(jnp.float32)
        offset = (y_cells[None, :] - y_start[:, None]) * 16.0 / y_count
        prof_y = jnp.exp(-(offset * offset))
        scale = 0.5 * (1.0 + power_level)
        thermal = thermal + DT * (
            flux
            + scale[:, None, None, None] * prof_y[:, None, :, None] * prof_z[None, None, None, :]
        )
    adjoint = weights
    gradient = jnp.zeros(conductivity.shape, jnp.float32)
    for index_step in reversed(range(STEPS)):
        padded_temp, padded_coef = saved[index_step]
        adj_ext = with_halo(adjoint, (("space", 1),), 1)
        padded_adj = pad_cross(adj_ext)
        centre_temp = padded_temp[:, 1:-1, 1:-1, 1:-1]
        centre_coef = padded_coef[:, 1:-1, 1:-1, 1:-1]
        grad_temp = adjoint
        grad_coef = jnp.zeros_like(adjoint)
        for near_temp, near_coef, near_adj in zip(
            neighbours(padded_temp), neighbours(padded_coef), neighbours(padded_adj)
        ):
            grad_temp = grad_temp + DT * 0.5 * (centre_coef + near_coef) * (near_adj - adjoint)
            grad_coef = grad_coef + 0.5 * DT * (near_temp - centre_temp) * (adjoint - near_adj)
        gradient = gradient + jnp.sum(grad_coef * conduct(centre_temp), axis=0)
        adjoint = grad_temp + grad_coef * kappa * conduct_slope(centre_temp)
    owned = lax.psum_scatter(gradient, "set", scatter_dimension=1, tiled=True)
    return (thermal, owned)


def solution(mesh):
    in_specs = (
        P("set", "space", None, None),
        P("space", None, None),
        P("set", "space", None, None),
        P("set"),
        P(),
        P(),
    )
    out_specs = (P("set", "space", None, None), P("space", "set", None))
    return jax.shard_map(local, mesh=mesh, in_specs=in_specs, out_specs=out_specs, check_vma=False)
```

profile of v0, /device:TPU:8, one launch (start us, length us, event | category | flops | bytes accessed | tf_op | source)
XLA Modules:
  0.0 302.1 jit_solution(13668709459791797471)
XLA Ops:
  7.2 2.3 multiply_bitcast_fusion.3
  9.8 1.9 collective-permute-start
  11.7 5.8 %collective-permute-start.1 = (f32[2,2,1,256,128]{4,3,2,1,0:T(8,128)S(1)}, f32[2,2,1,256,128]{4,3,2,1,0:T(8,128)S(1)}, u32[]{:S(2)}, u32[]{:S(2)}) collective-permute-start(f32[2,2,1,256,128]{4,3,2,1,0:T(8,128)S(1)} %get-tuple-element.39), channel_id=1, source_target_pairs={{8,0},{16,8},{24,16},{32,24},{40,32},{48,40},{56,48},{64,56},{72,6... | collective-permute-start | bytes 1572872 | tf_op jit(solution)/shard_map/ppermute | solution.py:20
  17.7 0.3 convert_reduce_fusion
  18.1 0.3 broadcast_multiply_fusion
  18.5 3.9 %collective-permute-done = f32[2,2,1,256,128]{4,3,2,1,0:T(8,128)S(1)} collective-permute-done((f32[2,2,1,256,128]{4,3,2,1,0:T(8,128)S(1)}, f32[2,2,1,256,128]{4,3,2,1,0:T(8,128)S(1)}, u32[]{:S(2)}, u32[]{:S(2)}) %collective-permute-start) | collective-permute-done | bytes 524320 | tf_op jit(solution)/shard_map/ppermute | solution.py:19
  22.4 1.8 collective-permute-done.1
  24.1 0.5 pad_maximum_fusion
  24.6 0.6 slice_bitcast_fusion.7
  25.2 0.6 copy-done.7
  25.9 3.7 %multiply_bitcast_fusion.2 = (f32[1,2,8,256,128]{4,3,2,1,0:T(8,128)S(1)}, f32[2,8,256,128]{3,2,1,0:T(8,128)S(1)}) fusion(f32[8,256,128]{2,1,0:T(8,128)S(1)} %copy-done.7, f32[2,8,256,128]{3,2,1,0:T(8,128)S(1)} %copy-done.12, f32[2,256,128]{2,1,0:T(8,128)S(1)} %get-tuple-element.55, f32[2,10,256,128]{3,2,1,0:T(8,128)S(1)} %get-tuple-element.31, ...), kind=kLoop, calls=%fused_computation.207 | loop fusion | flops 18874368 | bytes 23330816 | tf_op jit(solution)/shard_map/stack | solution.py:65
  29.6 2.0 collective-permute-start.2
  31.6 5.9 %collective-permute-start.3 = (f32[2,2,1,256,128]{4,3,2,1,0:T(8,128)S(1)}, f32[2,2,1,256,128]{4,3,2,1,0:T(8,128)S(1)}, u32[]{:S(2)}, u32[]{:S(2)}) collective-permute-start(f32[2,2,1,256,128]{4,3,2,1,0:T(8,128)S(1)} %get-tuple-element.37), channel_id=1, source_target_pairs={{8,0},{16,8},{24,16},{32,24},{40,32},{48,40},{56,48},{64,56},{72,6... | collective-permute-start | bytes 1572872 | tf_op jit(solution)/shard_map/ppermute | solution.py:20
  37.5 4.9 %collective-permute-done.2 = f32[2,2,1,256,128]{4,3,2,1,0:T(8,128)S(1)} collective-permute-done((f32[2,2,1,256,128]{4,3,2,1,0:T(8,128)S(1)}, f32[2,2,1,256,128]{4,3,2,1,0:T(8,128)S(1)}, u32[]{:S(2)}, u32[]{:S(2)}) %collective-permute-start.2) | collective-permute-done | bytes 524320 | tf_op jit(solution)/shard_map/ppermute | solution.py:19
  42.4 1.8 collective-permute-done.3
  44.1 0.6 pad_maximum_fusion.1
  44.8 0.4 slice_bitcast_fusion.5
  45.1 3.7 %multiply_bitcast_fusion.1 = (f32[1,2,8,256,128]{4,3,2,1,0:T(8,128)S(1)}, f32[2,8,256,128]{3,2,1,0:T(8,128)S(1)}) fusion(f32[8,256,128]{2,1,0:T(8,128)S(1)} %copy-done.7, f32[2,8,256,128]{3,2,1,0:T(8,128)S(1)} %get-tuple-element.23, f32[2,256,128]{2,1,0:T(8,128)S(1)} %get-tuple-element.53, f32[2,10,256,128]{3,2,1,0:T(8,128)S(1)} %get-tuple-element.29, ...), kind=kLoop, calls=%fused_computation.205 | loop fusion | flops 18874368 | bytes 23330816 | tf_op jit(solution)/shard_map/stack | solution.py:65
  48.9 2.1 collective-permute-start.4
  51.0 5.9 %collective-permute-start.5 = (f32[2,2,1,256,128]{4,3,2,1,0:T(8,128)S(1)}, f32[2,2,1,256,128]{4,3,2,1,0:T(8,128)S(1)}, u32[]{:S(2)}, u32[]{:S(2)}) collective-permute-start(f32[2,2,1,256,128]{4,3,2,1,0:T(8,128)S(1)} %get-tuple-element.35), channel_id=1, source_target_pairs={{8,0},{16,8},{24,16},{32,24},{40,32},{48,40},{56,48},{64,56},{72,6... | collective-permute-start | bytes 1572872 | tf_op jit(solution)/shard_map/ppermute | solution.py:20
  56.9 0.9 fusion.124
  57.8 2.4 collective-permute-start.8
  60.2 1.9 collective-permute-start.9
  62.1 1.4 collective-permute-done.5
  63.6 0.5 pad_maximum_fusion.2
  64.1 0.6 slice_bitcast_fusion.3
  64.7 5.0 %multiply_bitcast_fusion = (f32[1,2,8,256,128]{4,3,2,1,0:T(8,128)}, f32[2,8,256,128]{3,2,1,0:T(8,128)S(1)}) fusion(f32[8,256,128]{2,1,0:T(8,128)S(1)} %copy-done.7, f32[2,8,256,128]{3,2,1,0:T(8,128)S(1)} %get-tuple-element.21, f32[2,256,128]{2,1,0:T(8,128)S(1)} %get-tuple-element.54, f32[2,10,256,128]{3,2,1,0:T(8,128)S(1)} %get-tuple-element.27, ...), kind=kLoop, calls=%fused_computation.203 | loop fusion | flops 18874368 | bytes 23330816 | tf_op jit(solution)/shard_map/stack | solution.py:65
  69.7 1.5 pad_maximum_fusion.13
  71.2 1.9 collective-permute-start.6
  73.1 6.2 %collective-permute-start.7 = (f32[2,2,1,256,128]{4,3,2,1,0:T(8,128)S(1)}, f32[2,2,1,256,128]{4,3,2,1,0:T(8,128)S(1)}, u32[]{:S(2)}, u32[]{:S(2)}) collective-permute-start(f32[2,2,1,256,128]{4,3,2,1,0:T(8,128)S(1)} %get-tuple-element.33), channel_id=1, source_target_pairs={{8,0},{16,8},{24,16},{32,24},{40,32},{48,40},{56,48},{64,56},{72,6... | collective-permute-start | bytes 1572872 | tf_op jit(solution)/shard_map/ppermute | solution.py:20
  79.4 3.8 %select_maximum_fusion.6 = f32[2,10,258,130]{3,2,1,0:T(8,128)} fusion(f32[2,1,256,128]{3,2,1,0:T(8,128)S(1)} %collective-permute-done.8, f32[2,8,256,128]{3,2,1,0:T(8,128)S(1)} %copy-done.14, f32[2,1,256,128]{3,2,1,0:T(8,128)S(1)} %collective-permute-done.9), kind=kLoop, calls=%fused_computation.42 | loop fusion | flops 10062000 | bytes 5304640 | tf_op jit(solution)/shard_map/concatenate | solution.py:21
  83.2 0.7 collective-permute-done.6
  84.0 1.9 collective-permute-done.7
  85.9 0.5 pad_maximum_fusion.3
  86.4 0.3 slice_bitcast_fusion.1
  86.7 1.9 copy-done.15
  88.6 11.1 %multiply_reduce_fusion.2 = (f32[8,256,128]{2,1,0:T(8,128)}, f32[2,8,256,128]{3,2,1,0:T(8,128)}) fusion(f32[2,10,256,128]{3,2,1,0:T(8,128)S(1)} %get-tuple-element.25, f32[2,8,256,128]{3,2,1,0:T(8,128)S(1)} %copy-done.15, f32[2,10,258,130]{3,2,1,0:T(8,128)} %select_maximum_fusion.6, f32[2,1,256,128]{3,2,1,0:T(8,128)S(1)} %collective-permute-done.9, ...), kind=kLoop, calls=%fused_computation.200 | loop fusion | flops 18612224 | bytes 23068672 | tf_op jit(solution)/shard_map/reduce_sum | solution.py:99
  99.7 11.9 %fusion.4 = f32[2,8,256,128]{3,2,1,0:T(8,128)} fusion(f32[2,8,256,128]{3,2,1,0:T(8,128)} %param.8, f32[2,1,256,128]{3,2,1,0:T(8,128)S(1)} %collective-permute-done.9, f32[2,1,256,128]{3,2,1,0:T(8,128)S(1)} %collective-permute-done.8, f32[2,8,256,128]{3,2,1,0:T(8,128)} %get-tuple-element.15, f32[2,10,258,130]{3,2,1,0:T(8,128)} %select_maximum_fusion.6, ...), kind=kLoop, calls=%fused_computation.63 | loop fusion | flops 21495808 | bytes 27262976 | tf_op jit(solution)/shard_map/add | solution.py:100
  111.6 1.1 fusion.123
  112.6 5.9 %collective-permute-start.10 = (f32[2,1,256,128]{3,2,1,0:T(8,128)S(1)}, f32[2,1,256,128]{3,2,1,0:T(8,128)S(1)}, u32[]{:S(2)}, u32[]{:S(2)}) collective-permute-start(f32[2,1,256,128]{3,2,1,0:T(8,128)S(1)} %get-tuple-element.44), channel_id=1, source_target_pairs={{8,0},{16,8},{24,16},{32,24},{40,32},{48,40},{56,48},{64,56},{72,6... | collective-permute-start | bytes 786440 | tf_op jit(solution)/shard_map/ppermute | solution.py:20
  118.6 2.4 collective-permute-start.11
  121.0 1.4 collective-permute-done.10
  122.4 6.2 %collective-permute-done.11 = f32[2,1,256,128]{3,2,1,0:T(8,128)S(1)} collective-permute-done((f32[2,1,256,128]{3,2,1,0:T(8,128)S(1)}, f32[2,1,256,128]{3,2,1,0:T(8,128)S(1)}, u32[]{:S(2)}, u32[]{:S(2)}) %collective-permute-start.11) | collective-permute-done | bytes 262176 | tf_op jit(solution)/shard_map/ppermute | solution.py:19
  128.6 5.0 %select_maximum_fusion.4 = f32[2,10,258,130]{3,2,1,0:T(8,128)} fusion(f32[2,1,256,128]{3,2,1,0:T(8,128)S(1)} %collective-permute-done.10, f32[2,8,256,128]{3,2,1,0:T(8,128)} %fusion.4, f32[2,1,256,128]{3,2,1,0:T(8,128)S(1)} %collective-permute-done.11), kind=kLoop, calls=%fused_computation.40 | loop fusion | flops 10062000 | bytes 5304640 | tf_op jit(solution)/shard_map/concatenate | solution.py:21
  133.7 11.2 %multiply_reduce_fusion.1 = (f32[8,256,128]{2,1,0:T(8,128)}, f32[2,8,256,128]{3,2,1,0:T(8,128)}) fusion(f32[2,10,256,128]{3,2,1,0:T(8,128)S(1)} %copy-done.4, f32[2,8,256,128]{3,2,1,0:T(8,128)S(1)} %copy-done.10, f32[2,10,258,130]{3,2,1,0:T(8,128)} %select_maximum_fusion.4, f32[2,1,256,128]{3,2,1,0:T(8,128)S(1)} %collective-permute-done.11, ...), kind=kLoop, calls=%fused_computation.198 | loop fusion | flops 18612224 | bytes 23068672 | tf_op jit(solution)/shard_map/reduce_sum | solution.py:99
  144.9 12.5 %fusion.6 = f32[2,8,256,128]{3,2,1,0:T(8,128)} fusion(f32[2,8,256,128]{3,2,1,0:T(8,128)} %fusion.4, f32[2,1,256,128]{3,2,1,0:T(8,128)S(1)} %collective-permute-done.11, f32[2,1,256,128]{3,2,1,0:T(8,128)S(1)} %collective-permute-done.10, f32[2,8,256,128]{3,2,1,0:T(8,128)} %get-tuple-element.13, f32[2,10,258,130]{3,2,1,0:T(8,128)} %select_maximum_fusion.4, ...), kind=kLoop, calls=%fused_computation.65 | loop fusion | flops 21495808 | bytes 27262976 | tf_op jit(solution)/shard_map/add | solution.py:100
  157.4 1.1 fusion.122
  158.5 1.9 collective-permute-start.12
  160.4 2.5 collective-permute-start.13
  162.9 1.3 collective-permute-done.12
  164.3 6.1 %collective-permute-done.13 = f32[2,1,256,128]{3,2,1,0:T(8,128)S(1)} collective-permute-done((f32[2,1,256,128]{3,2,1,0:T(8,128)S(1)}, f32[2,1,256,128]{3,2,1,0:T(8,128)S(1)}, u32[]{:S(2)}, u32[]{:S(2)}) %collective-permute-start.13) | collective-permute-done | bytes 262176 | tf_op jit(solution)/shard_map/ppermute | solution.py:19
  170.3 5.0 %select_maximum_fusion.2 = f32[2,10,258,130]{3,2,1,0:T(8,128)} fusion(f32[2,1,256,128]{3,2,1,0:T(8,128)S(1)} %collective-permute-done.12, f32[2,8,256,128]{3,2,1,0:T(8,128)} %fusion.6, f32[2,1,256,128]{3,2,1,0:T(8,128)S(1)} %collective-permute-done.13), kind=kLoop, calls=%fused_computation.38 | loop fusion | flops 10062000 | bytes 5304640 | tf_op jit(solution)/shard_map/concatenate | solution.py:21
  175.4 10.2 %multiply_reduce_fusion = (f32[8,256,128]{2,1,0:T(8,128)S(1)}, f32[2,8,256,128]{3,2,1,0:T(8,128)}) fusion(f32[2,10,256,128]{3,2,1,0:T(8,128)S(1)} %get-tuple-element.29, f32[2,8,256,128]{3,2,1,0:T(8,128)S(1)} %copy-done.9, f32[2,10,258,130]{3,2,1,0:T(8,128)} %select_maximum_fusion.2, f32[2,1,256,128]{3,2,1,0:T(8,128)S(1)} %collective-permute-done.13, ...), kind=kLoop, calls=%fused_computation.196 | loop fusion | flops 18612224 | bytes 23068672 | tf_op jit(solution)/shard_map/reduce_sum | solution.py:99
  185.5 11.8 %fusion.8 = f32[2,8,256,128]{3,2,1,0:T(8,128)} fusion(f32[2,8,256,128]{3,2,1,0:T(8,128)} %fusion.6, f32[2,1,256,128]{3,2,1,0:T(8,128)S(1)} %collective-permute-done.13, f32[2,1,256,128]{3,2,1,0:T(8,128)S(1)} %collective-permute-done.12, f32[2,8,256,128]{3,2,1,0:T(8,128)} %get-tuple-element.17, f32[2,10,258,130]{3,2,1,0:T(8,128)} %select_maximum_fusion.2, ...), kind=kLoop, calls=%fused_computation.67 | loop fusion | flops 21495808 | bytes 27262976 | tf_op jit(solution)/shard_map/add | solution.py:100
  197.3 1.1 fusion.121
  198.4 1.9 collective-permute-start.15
  200.3 6.3 %collective-permute-start.14 = (f32[2,1,256,128]{3,2,1,0:T(8,128)S(1)}, f32[2,1,256,128]{3,2,1,0:T(8,128)S(1)}, u32[]{:S(2)}, u32[]{:S(2)}) collective-permute-start(f32[2,1,256,128]{3,2,1,0:T(8,128)S(1)} %get-tuple-element.41), channel_id=1, source_target_pairs={{8,0},{16,8},{24,16},{32,24},{40,32},{48,40},{56,48},{64,56},{72,6... | collective-permute-start | bytes 786440 | tf_op jit(solution)/shard_map/ppermute | solution.py:20
  206.6 1.6 collective-permute-done.15
  208.2 2.0 collective-permute-done.14
  210.2 3.5 %select_maximum_fusion = f32[2,10,258,130]{3,2,1,0:T(8,128)S(1)} fusion(f32[2,1,256,128]{3,2,1,0:T(8,128)S(1)} %collective-permute-done.14, f32[2,8,256,128]{3,2,1,0:T(8,128)} %fusion.8, f32[2,1,256,128]{3,2,1,0:T(8,128)S(1)} %collective-permute-done.15), kind=kLoop, calls=%fused_computation.36 | loop fusion | flops 10062000 | bytes 5304640 | tf_op jit(solution)/shard_map/concatenate | solution.py:21
  213.8 5.3 %fusion.43 = f32[8,256,128]{2,1,0:T(8,128)} fusion(f32[2,8,256,128]{3,2,1,0:T(8,128)S(1)} %copy-done.13, f32[2,10,258,130]{3,2,1,0:T(8,128)S(1)} %select_maximum_fusion, f32[2,1,256,128]{3,2,1,0:T(8,128)S(1)} %collective-permute-done.15, f32[2,1,256,128]{3,2,1,0:T(8,128)S(1)} %collective-permute-done.14, f32[2,10,256,128]{3,2,1,0:T(8,128)S(1)} %copy-done.6), kind=kLoop, calls=%fused_computation.103 | loop fusion | flops 18612224 | bytes 20971520 | tf_op jit(solution)/shard_map/reduce_sum | solution.py:99
  219.1 2.5 add_add_fusion
  221.6 10.6 %multiply_add_fusion = f32[2,8,256,128]{3,2,1,0:T(8,128)} fusion(f32[2,8,256,128]{3,2,1,0:T(8,128)} %copy-done.11, f32[2,10,256,128]{3,2,1,0:T(8,128)} %copy-done, f32[2,256,128]{2,1,0:T(8,128)S(1)} %get-tuple-element.52, f32[2,10,256,128]{3,2,1,0:T(8,128)S(1)} %get-tuple-element.24), kind=kLoop, calls=%fused_computation.202 | loop fusion | flops 16777216 | bytes 20185088 | tf_op jit(solution)/shard_map/add | solution.py:80
  232.2 63.0 %reduce-scatter.2.cloned.1.call-done = f32[8,32,128]{2,1,0:T(8,128)} async-done(((f32[8,256,128]{2,1,0:T(8,128)}), f32[8,32,128]{2,1,0:T(8,128)}) %reduce-scatter.2.cloned.1.call-update) | async-done | bytes 131088 | tf_op jit(solution)/shard_map/reduce_scatter | solution.py:101
  (55 shorter events, 0.9 us)
Async XLA Ops:
  7.2 2.5 copy-start.12
  7.2 288.0 %reduce-scatter.2.cloned.1.call-start = ((), (), s32[]{:S(2)}) async-start(), calls=%async_computation.1 | async-start | bytes 1179648 | tf_op jit(solution)/shard_map/reduce_scatter | solution.py:101
  9.7 7.8 %copy-start.21 = (s32[2]{0:T(128)S(1)}, s32[2]{0:T(128)}, u32[]{:S(2)}) copy-start(s32[2]{0:T(128)} %param.9) | copy-start | bytes 28
  9.7 7.9 %copy-start.19 = (s32[64,4]{0,1:T(4,128)S(1)}, s32[64,4]{0,1:T(4,128)}, u32[]{:S(2)}) copy-start(s32[64,4]{0,1:T(4,128)} %param.10) | copy-start | bytes 3076
  9.7 7.9 %copy-start.20 = (s32[64,4]{0,1:T(4,128)S(1)}, s32[64,4]{0,1:T(4,128)}, u32[]{:S(2)}) copy-start(s32[64,4]{0,1:T(4,128)} %param.11) | copy-start | bytes 3076
  9.8 12.6 %collective-permute-start = (f32[2,2,1,256,128]{4,3,2,1,0:T(8,128)S(1)}, f32[2,2,1,256,128]{4,3,2,1,0:T(8,128)S(1)}, u32[]{:S(2)}, u32[]{:S(2)}) collective-permute-start(f32[2,2,1,256,128]{4,3,2,1,0:T(8,128)S(1)} %get-tuple-element.38), channel_id=1, source_target_pairs={{0,8},{8,16},{16,24},{24,32},{32,40},{40,48},{48,56},{56,64},{64,7... | collective-permute-start | bytes 1572872 | tf_op jit(solution)/shard_map/ppermute | solution.py:19
  11.7 12.4 %collective-permute-start.1 = (f32[2,2,1,256,128]{4,3,2,1,0:T(8,128)S(1)}, f32[2,2,1,256,128]{4,3,2,1,0:T(8,128)S(1)}, u32[]{:S(2)}, u32[]{:S(2)}) collective-permute-start(f32[2,2,1,256,128]{4,3,2,1,0:T(8,128)S(1)} %get-tuple-element.39), channel_id=1, source_target_pairs={{8,0},{16,8},{24,16},{32,24},{40,32},{48,40},{56,48},{64,56},{72,6... | collective-permute-start | bytes 1572872 | tf_op jit(solution)/shard_map/ppermute | solution.py:20
  24.6 1.2 copy-start.7
  25.2 4.3 %copy-start.5 = (f32[2,10,256,128]{3,2,1,0:T(8,128)}, f32[2,10,256,128]{3,2,1,0:T(8,128)S(1)}, u32[]{:S(2)}) copy-start(f32[2,10,256,128]{3,2,1,0:T(8,128)S(1)} %get-tuple-element.31) | copy-start | bytes 7864324
  29.6 12.8 %collective-permute-start.2 = (f32[2,2,1,256,128]{4,3,2,1,0:T(8,128)S(1)}, f32[2,2,1,256,128]{4,3,2,1,0:T(8,128)S(1)}, u32[]{:S(2)}, u32[]{:S(2)}) collective-permute-start(f32[2,2,1,256,128]{4,3,2,1,0:T(8,128)S(1)} %get-tuple-element.36), channel_id=1, source_target_pairs={{0,8},{8,16},{16,24},{24,32},{32,40},{40,48},{48,56},{56,64},{64,7... | collective-permute-start | bytes 1572872 | tf_op jit(solution)/shard_map/ppermute | solution.py:19
  31.6 12.5 %collective-permute-start.3 = (f32[2,2,1,256,128]{4,3,2,1,0:T(8,128)S(1)}, f32[2,2,1,256,128]{4,3,2,1,0:T(8,128)S(1)}, u32[]{:S(2)}, u32[]{:S(2)}) collective-permute-start(f32[2,2,1,256,128]{4,3,2,1,0:T(8,128)S(1)} %get-tuple-element.37), channel_id=1, source_target_pairs={{8,0},{16,8},{24,16},{32,24},{40,32},{48,40},{56,48},{64,56},{72,6... | collective-permute-start | bytes 1572872 | tf_op jit(solution)/shard_map/ppermute | solution.py:20
  48.8 8.1 %copy-start.14 = (f32[2,8,256,128]{3,2,1,0:T(8,128)S(1)}, f32[2,8,256,128]{3,2,1,0:T(8,128)}, u32[]{:S(2)}) copy-start(f32[2,8,256,128]{3,2,1,0:T(8,128)} %param.8) | copy-start | bytes 6291460
  48.9 13.2 %collective-permute-start.4 = (f32[2,2,1,256,128]{4,3,2,1,0:T(8,128)S(1)}, f32[2,2,1,256,128]{4,3,2,1,0:T(8,128)S(1)}, u32[]{:S(2)}, u32[]{:S(2)}) collective-permute-start(f32[2,2,1,256,128]{4,3,2,1,0:T(8,128)S(1)} %get-tuple-element.34), channel_id=1, source_target_pairs={{0,8},{8,16},{16,24},{24,32},{32,40},{40,48},{48,56},{56,64},{64,7... | collective-permute-start | bytes 1572872 | tf_op jit(solution)/shard_map/ppermute | solution.py:19
  51.0 12.6 %collective-permute-start.5 = (f32[2,2,1,256,128]{4,3,2,1,0:T(8,128)S(1)}, f32[2,2,1,256,128]{4,3,2,1,0:T(8,128)S(1)}, u32[]{:S(2)}, u32[]{:S(2)}) collective-permute-start(f32[2,2,1,256,128]{4,3,2,1,0:T(8,128)S(1)} %get-tuple-element.35), channel_id=1, source_target_pairs={{8,0},{16,8},{24,16},{32,24},{40,32},{48,40},{56,48},{64,56},{72,6... | collective-permute-start | bytes 1572872 | tf_op jit(solution)/shard_map/ppermute | solution.py:20
  57.8 21.6 %collective-permute-start.8 = (f32[2,1,256,128]{3,2,1,0:T(8,128)}, f32[2,1,256,128]{3,2,1,0:T(8,128)S(1)}, u32[]{:S(2)}, u32[]{:S(2)}) collective-permute-start(f32[2,1,256,128]{3,2,1,0:T(8,128)} %get-tuple-element.46), channel_id=1, source_target_pairs={{8,0},{16,8},{24,16},{32,24},{40,32},{48,40},{56,48},{64,56},{72,6... | collective-permute-start | bytes 786440 | tf_op jit(solution)/shard_map/ppermute | solution.py:20
  60.2 19.2 %collective-permute-start.9 = (f32[2,1,256,128]{3,2,1,0:T(8,128)}, f32[2,1,256,128]{3,2,1,0:T(8,128)S(1)}, u32[]{:S(2)}, u32[]{:S(2)}) collective-permute-start(f32[2,1,256,128]{3,2,1,0:T(8,128)} %get-tuple-element.47), channel_id=1, source_target_pairs={{0,8},{8,16},{16,24},{24,32},{32,40},{40,48},{48,56},{56,64},{64,7... | collective-permute-start | bytes 786440 | tf_op jit(solution)/shard_map/ppermute | solution.py:19
  64.6 5.1 %copy-start.1 = (f32[2,10,256,128]{3,2,1,0:T(8,128)}, f32[2,10,256,128]{3,2,1,0:T(8,128)S(1)}, u32[]{:S(2)}) copy-start(f32[2,10,256,128]{3,2,1,0:T(8,128)S(1)} %get-tuple-element.26) | copy-start | bytes 7864324
  64.7 5.1 %copy-start.3 = (f32[2,10,256,128]{3,2,1,0:T(8,128)}, f32[2,10,256,128]{3,2,1,0:T(8,128)S(1)}, u32[]{:S(2)}) copy-start(f32[2,10,256,128]{3,2,1,0:T(8,128)S(1)} %get-tuple-element.27) | copy-start | bytes 7864324
  69.7 16.2 %copy-start.11 = (f32[2,8,256,128]{3,2,1,0:T(8,128)}, f32[2,8,256,128]{3,2,1,0:T(8,128)S(1)}, u32[]{:S(2)}) copy-start(f32[2,8,256,128]{3,2,1,0:T(8,128)S(1)} %get-tuple-element.19) | copy-start | bytes 6291460
  71.2 12.8 %collective-permute-start.6 = (f32[2,2,1,256,128]{4,3,2,1,0:T(8,128)S(1)}, f32[2,2,1,256,128]{4,3,2,1,0:T(8,128)S(1)}, u32[]{:S(2)}, u32[]{:S(2)}) collective-permute-start(f32[2,2,1,256,128]{4,3,2,1,0:T(8,128)S(1)} %get-tuple-element.32), channel_id=1, source_target_pairs={{0,8},{8,16},{16,24},{24,32},{32,40},{40,48},{48,56},{56,64},{64,7... | collective-permute-start | bytes 1572872 | tf_op jit(solution)/shard_map/ppermute | solution.py:19
  73.1 12.8 %copy-start.16 = (f32[1,2,8,256,128]{4,3,2,1,0:T(8,128)S(1)}, f32[1,2,8,256,128]{4,3,2,1,0:T(8,128)}, u32[]{:S(2)}) copy-start(f32[1,2,8,256,128]{4,3,2,1,0:T(8,128)} %get-tuple-element.18) | copy-start | bytes 6291460
  73.1 12.7 %collective-permute-start.7 = (f32[2,2,1,256,128]{4,3,2,1,0:T(8,128)S(1)}, f32[2,2,1,256,128]{4,3,2,1,0:T(8,128)S(1)}, u32[]{:S(2)}, u32[]{:S(2)}) collective-permute-start(f32[2,2,1,256,128]{4,3,2,1,0:T(8,128)S(1)} %get-tuple-element.33), channel_id=1, source_target_pairs={{8,0},{16,8},{24,16},{32,24},{40,32},{48,40},{56,48},{64,56},{72,6... | collective-permute-start | bytes 1572872 | tf_op jit(solution)/shard_map/ppermute | solution.py:20
  86.4 2.2 copy-start.15
  86.7 13.0 %copy-start = (f32[2,10,256,128]{3,2,1,0:T(8,128)}, f32[2,10,256,128]{3,2,1,0:T(8,128)S(1)}, u32[]{:S(2)}) copy-start(f32[2,10,256,128]{3,2,1,0:T(8,128)S(1)} %get-tuple-element.25) | copy-start | bytes 7864324
  112.6 9.8 %collective-permute-start.10 = (f32[2,1,256,128]{3,2,1,0:T(8,128)S(1)}, f32[2,1,256,128]{3,2,1,0:T(8,128)S(1)}, u32[]{:S(2)}, u32[]{:S(2)}) collective-permute-start(f32[2,1,256,128]{3,2,1,0:T(8,128)S(1)} %get-tuple-element.44), channel_id=1, source_target_pairs={{8,0},{16,8},{24,16},{32,24},{40,32},{48,40},{56,48},{64,56},{72,6... | collective-permute-start | bytes 786440 | tf_op jit(solution)/shard_map/ppermute | solution.py:20
  118.6 15.1 %copy-start.4 = (f32[2,10,256,128]{3,2,1,0:T(8,128)S(1)}, f32[2,10,256,128]{3,2,1,0:T(8,128)}, u32[]{:S(2)}) copy-start(f32[2,10,256,128]{3,2,1,0:T(8,128)} %copy-done.3) | copy-start | bytes 7864324
  118.6 15.1 %copy-start.10 = (f32[2,8,256,128]{3,2,1,0:T(8,128)S(1)}, f32[2,8,256,128]{3,2,1,0:T(8,128)}, u32[]{:S(2)}) copy-start(f32[2,8,256,128]{3,2,1,0:T(8,128)} %fusion.4) | copy-start | bytes 6291460
  118.6 10.1 %collective-permute-start.11 = (f32[2,1,256,128]{3,2,1,0:T(8,128)S(1)}, f32[2,1,256,128]{3,2,1,0:T(8,128)S(1)}, u32[]{:S(2)}, u32[]{:S(2)}) collective-permute-start(f32[2,1,256,128]{3,2,1,0:T(8,128)S(1)} %get-tuple-element.45), channel_id=1, source_target_pairs={{0,8},{8,16},{16,24},{24,32},{32,40},{40,48},{48,56},{56,64},{64,7... | collective-permute-start | bytes 786440 | tf_op jit(solution)/shard_map/ppermute | solution.py:19
  133.7 11.2 %copy-start.2 = (f32[2,10,256,128]{3,2,1,0:T(8,128)S(1)}, f32[2,10,256,128]{3,2,1,0:T(8,128)}, u32[]{:S(2)}) copy-start(f32[2,10,256,128]{3,2,1,0:T(8,128)} %copy-done.1) | copy-start | bytes 7864324
  158.5 5.8 %collective-permute-start.12 = (f32[2,1,256,128]{3,2,1,0:T(8,128)S(1)}, f32[2,1,256,128]{3,2,1,0:T(8,128)S(1)}, u32[]{:S(2)}, u32[]{:S(2)}) collective-permute-start(f32[2,1,256,128]{3,2,1,0:T(8,128)S(1)} %get-tuple-element.42), channel_id=1, source_target_pairs={{8,0},{16,8},{24,16},{32,24},{40,32},{48,40},{56,48},{64,56},{72,6... | collective-permute-start | bytes 786440 | tf_op jit(solution)/shard_map/ppermute | solution.py:20
  160.4 15.0 %copy-start.9 = (f32[2,8,256,128]{3,2,1,0:T(8,128)S(1)}, f32[2,8,256,128]{3,2,1,0:T(8,128)}, u32[]{:S(2)}) copy-start(f32[2,8,256,128]{3,2,1,0:T(8,128)} %fusion.6) | copy-start | bytes 6291460
  160.4 9.9 %collective-permute-start.13 = (f32[2,1,256,128]{3,2,1,0:T(8,128)S(1)}, f32[2,1,256,128]{3,2,1,0:T(8,128)S(1)}, u32[]{:S(2)}, u32[]{:S(2)}) collective-permute-start(f32[2,1,256,128]{3,2,1,0:T(8,128)S(1)} %get-tuple-element.43), channel_id=1, source_target_pairs={{0,8},{8,16},{16,24},{24,32},{32,40},{40,48},{48,56},{56,64},{64,7... | collective-permute-start | bytes 786440 | tf_op jit(solution)/shard_map/ppermute | solution.py:19
  175.4 10.2 %copy-start.8 = (f32[8,256,128]{2,1,0:T(8,128)S(1)}, f32[8,256,128]{2,1,0:T(8,128)}, u32[]{:S(2)}) copy-start(f32[8,256,128]{2,1,0:T(8,128)} %param.7) | copy-start | bytes 3145732
  198.4 9.8 %collective-permute-start.15 = (f32[2,1,256,128]{3,2,1,0:T(8,128)S(1)}, f32[2,1,256,128]{3,2,1,0:T(8,128)S(1)}, u32[]{:S(2)}, u32[]{:S(2)}) collective-permute-start(f32[2,1,256,128]{3,2,1,0:T(8,128)S(1)} %get-tuple-element.40), channel_id=1, source_target_pairs={{0,8},{8,16},{16,24},{24,32},{32,40},{40,48},{48,56},{56,64},{64,7... | collective-permute-start | bytes 786440 | tf_op jit(solution)/shard_map/ppermute | solution.py:19
  200.3 13.4 %copy-start.6 = (f32[2,10,256,128]{3,2,1,0:T(8,128)S(1)}, f32[2,10,256,128]{3,2,1,0:T(8,128)}, u32[]{:S(2)}) copy-start(f32[2,10,256,128]{3,2,1,0:T(8,128)} %copy-done.5) | copy-start | bytes 7864324
  200.3 13.4 %copy-start.13 = (f32[2,8,256,128]{3,2,1,0:T(8,128)S(1)}, f32[2,8,256,128]{3,2,1,0:T(8,128)}, u32[]{:S(2)}) copy-start(f32[2,8,256,128]{3,2,1,0:T(8,128)} %fusion.8) | copy-start | bytes 6291460
  200.3 9.9 %collective-permute-start.14 = (f32[2,1,256,128]{3,2,1,0:T(8,128)S(1)}, f32[2,1,256,128]{3,2,1,0:T(8,128)S(1)}, u32[]{:S(2)}, u32[]{:S(2)}) collective-permute-start(f32[2,1,256,128]{3,2,1,0:T(8,128)S(1)} %get-tuple-element.41), channel_id=1, source_target_pairs={{8,0},{16,8},{24,16},{32,24},{40,32},{48,40},{56,48},{64,56},{72,6... | collective-permute-start | bytes 786440 | tf_op jit(solution)/shard_map/ppermute | solution.py:20
  213.7 5.4 %copy-start.17 = (f32[8,256,128]{2,1,0:T(8,128)S(1)}, f32[8,256,128]{2,1,0:T(8,128)}, u32[]{:S(2)}) copy-start(f32[8,256,128]{2,1,0:T(8,128)} %get-tuple-element.14) | copy-start | bytes 3145732
  213.8 5.3 %copy-start.18 = (f32[8,256,128]{2,1,0:T(8,128)S(1)}, f32[8,256,128]{2,1,0:T(8,128)}, u32[]{:S(2)}) copy-start(f32[8,256,128]{2,1,0:T(8,128)} %get-tuple-element.12) | copy-start | bytes 3145732
Sparse Core Ops, SparseCore 0:
  221.8 73.4 reduce-scatter.1
where the time goes:
time: 304 us; the launch traced here: 302 us
  other arithmetic  124 us (41%)
  waiting for transfers between devices  98.1 us (32%)
  starting transfers between devices  57 us (19%)
  between operations  14.5 us (5%)
  local copies, waits for them, and re-layouts  8.71 us (3%)
    reduce_scatter x1, waiting for transfers between devices, local(): owned = lax.psum_scatter(gradient, 'set', scatter_dimension=1, tiled=True)  63 us
    ppermute x8, starting transfers between devices, with_halo(): after = lax.ppermute(initial, axis, down)  40.3 us
    reduce_sum x4, other arithmetic, local(): gradient = gradient + jnp.sum(grad_coef * conduct(centre_temp), axis=0)  37.8 us
    add x3, other arithmetic, local(): adjoint = grad_temp + grad_coef * kappa * conduct_slope(centre_temp)  36.1 us
    ppermute x8, waiting for transfers between devices, with_halo(): before = lax.ppermute(last, axis, up)  23.4 us
    concatenate x8, other arithmetic, with_halo(): shard = jnp.concatenate([before, shard, after], axis=dim)  19.5 us
    ppermute x8, starting transfers between devices, with_halo(): before = lax.ppermute(last, axis, up)  16.7 us
    another operation x4, other arithmetic, local(): stacked = with_halo(jnp.stack((thermal, coeffs)), (('space', 2),), 1)  14.7 us
  transfers between devices with their start and end apart: 17, of which 14 were waited for; matrix products, arithmetic and copies ran while one was open for 8% of the time, Pallas kernels for 0%

commit v1 on v0

v1 whole, which is shorter than its diff:
```python
import functools

import jax
import jax.numpy as jnp
from jax import lax
from jax.experimental import pallas as pl
from jax.experimental.pallas import tpu as pltpu
from jax.sharding import PartitionSpec as P

STEPS = 4
DT = 0.15
HALF = 0.5 * DT
BLOCKS = 8
LANES = 128
MESH = pl.DeviceIdType.MESH


def recip(value):
    return pl.reciprocal(value, approx=True)


def kernel(planes, inner, set_size, space_size, *refs):
    init_hbm, cond_hbm, weights_hbm, index_smem, track_smem, power_smem, final_hbm, grad_hbm = refs[:8]
    refs = list(refs[8:])

    def take(*shape):
        if not shape:
            return refs.pop(0)
        return [take(*shape[1:]) for _ in range(shape[0])]

    temp = take(STEPS + 1, 2)
    coef = take(STEPS, 2)
    az = take(STEPS, 2)
    dz = take(STEPS, 2)
    lam = take(2, 2)
    hz, hz_low, mz, mz_low = (take(2) for _ in range(4))
    kap, heat, acc, roll_u, roll_a = (take() for _ in range(5))
    share, inbox, inbox_y = (take() for _ in range(3))
    in_sem, out_sem, k_send, k_recv, u_send, u_recv, l_send, l_recv, g_sem, x_send, x_recv, y_send, y_recv = (
        take() for _ in range(13)
    )
    space = lax.axis_index("space")
    own_set = lax.axis_index("set")
    core = lax.rem(space, 2)
    top = core == 1
    edge = (jnp.where(top, planes, 1), jnp.where(top, 1, planes))
    halo = (jnp.where(top, planes + 1, 0), jnp.where(top, 0, planes + 1))
    there = (jnp.where(top, 0, planes + 1), jnp.where(top, planes + 1, 0))
    partner = (
        jnp.clip(jnp.where(top, space + 1, space - 1), 0, space_size - 1),
        jnp.where(top, space - 1, space + 1),
    )
    has_far = jnp.logical_and(space != 0, space != space_size - 1)
    lane = lax.broadcasted_iota(jnp.int32, (BLOCKS, LANES), 1)
    sub = lax.broadcasted_iota(jnp.int32, (BLOCKS, LANES), 0)
    not_last = lane < LANES - 1
    first_lane = lane == 0

    def relayout(src, dst, sem):
        return [
            pltpu.make_async_copy(
                src.at[:, pl.ds(b * inner, inner), :],
                dst.at[pl.ds(1, planes), :, b, :],
                sem.at[b],
            )
            for b in range(BLOCKS)
        ]

    loads = [
        relayout(init_hbm.at[0], temp[0][0], in_sem.at[0]),
        relayout(cond_hbm, kap, in_sem.at[1]),
        relayout(init_hbm.at[1], temp[0][1], in_sem.at[2]),
        relayout(weights_hbm.at[0], lam[0][0], in_sem.at[3]),
        relayout(weights_hbm.at[1], lam[0][1], in_sem.at[4]),
    ]
    for group in loads:
        for copy in group:
            copy.start()

    barrier = pltpu.get_barrier_semaphore()
    pl.semaphore_signal(barrier, inc=1, device_id=(partner[1], own_set), device_id_type=MESH)

    @pl.when(has_far)
    def _():
        pl.semaphore_signal(barrier, inc=1, device_id=(partner[0], own_set), device_id_type=MESH)

    own_y, own_x = own_set // 4, lax.rem(own_set, 4)
    x_right, x_left, x_far = (lax.rem(own_x + i, 4) for i in (1, 3, 2))
    set_right, set_left = own_y * 4 + x_right, own_y * 4 + x_left
    set_y = (1 - own_y) * 4 + own_x
    for other_set in (set_right, set_left, set_y):
        pl.semaphore_signal(barrier, inc=1, device_id=(space, other_set), device_id_type=MESH)

    def swap(ref, side, send, recv):
        return pltpu.make_async_remote_copy(
            src_ref=ref.at[edge[side]],
            dst_ref=ref.at[there[side]],
            send_sem=send,
            recv_sem=recv,
            device_id=(partner[side], own_set),
            device_id_type=MESH,
        )

    def move_temp(side, s, n):
        return swap(temp[n][s], side, u_send.at[side, s, n], u_recv.at[side, s, n])

    def move_lam(side, s, m):
        return swap(lam[m % 2][s], side, l_send.at[side, s, m], l_recv.at[side, s, m])

    def move_kap(side):
        return swap(kap, side, k_send.at[side], k_recv.at[side])

    def each_side(side, do):
        if side:
            do()
        else:
            pl.when(has_far)(do)

    @pl.when(jnp.logical_not(has_far))
    def _():
        zero = jnp.zeros((inner, BLOCKS, LANES), jnp.float32)
        kap[halo[0]] = zero
        for s in range(2):
            for n in range(STEPS):
                temp[n][s][halo[0]] = zero
            for n in range(2):
                lam[n][s][halo[0]] = zero

    prof_z = jnp.exp(-4.0 * lane.astype(jnp.float32) / LANES)

    def make_heat(i, carry):
        s = i // STEPS
        n = lax.rem(i, STEPS)
        row = index_smem[s]
        y0 = track_smem[row, n].astype(jnp.float32)
        level = power_smem[row, n].astype(jnp.float32)
        plane = prof_z * (DT * 0.5 * (1.0 + level))

        def rows(y, c):
            offset = ((sub * inner + y).astype(jnp.float32) - y0) * (16.0 / (inner * BLOCKS))
            heat[i, y] = plane * jnp.exp(-(offset * offset))
            return c

        return lax.fori_loop(0, inner, rows, carry, unroll=8)

    lax.fori_loop(0, 2 * STEPS, make_heat, 0)

    def clear(y, c):
        for p in range(planes):
            acc[p, y] = jnp.zeros((BLOCKS, LANES), jnp.float32)
        return c

    lax.fori_loop(0, inner, clear, 0)

    pl.semaphore_wait(barrier, jnp.where(has_far, 5, 4))

    for which, go in ((0, lambda side: move_temp(side, 0, 0)), (1, move_kap), (2, lambda side: move_temp(side, 1, 0))):
        for copy in loads[which]:
            copy.wait()
        for side in range(2):
            each_side(side, lambda go=go, side=side: go(side).start())

    def scale(p):
        for k in range(inner):
            kap[p, k] = HALF * kap[p, k]

    each_side(0, lambda: move_kap(0).wait_send())
    move_kap(1).wait_send()

    def scale_all(p, c):
        scale(p)
        return c

    lax.fori_loop(1, planes + 1, scale_all, 0)

    def wrapped(value, shift, last):
        return jnp.where(sub == last, 0.0, pltpu.roll(value, shift, 0))

    def before(rows):
        return [wrapped(rows[-1], 1, 0)] + rows[:-1]

    def load(ref, p):
        return [ref[p, k] for k in range(inner)]

    def shifted(value):
        return pltpu.roll(value, LANES - 1, 1)

    def spread_temp(s, n):
        u_ref, a_ref = temp[n][s], coef[n][s]

        def first(p, k):
            roll_u[k] = shifted(u_ref[p, k])
            roll_a[k] = shifted(a_ref[p, k])

        def second(p, k):
            u, a = u_ref[p, k], a_ref[p, k]
            face = a + jnp.where(not_last, roll_a[k], 0.0)
            diff = jnp.where(not_last, roll_u[k], 0.0) - u
            g = face * diff
            az[n][s][p - 1, k] = face
            dz[n][s][p - 1, k] = diff
            hz[s][p - 1, k] = g
            hz_low[s][p - 1, k] = pltpu.roll(g, 1, 1)

        return first, second

    def spread_lam(s, n, whole):
        v_ref = lam[(n + 1) % 2][s]

        def first(p, k):
            roll_u[k] = shifted(v_ref[p, k])

        def second(p, k):
            d = jnp.where(not_last, roll_u[k], 0.0) - v_ref[p, k]
            m = dz[n][s][p - 1, k] * d
            mz[s][p - 1, k] = m
            mz_low[s][p - 1, k] = pltpu.roll(m, 1, 1)
            if whole:
                h = az[n][s][p - 1, k] * d
                hz[s][p - 1, k] = h
                hz_low[s][p - 1, k] = pltpu.roll(h, 1, 1)

        return first, second

    def plane_coef(s, n, p):
        for k in range(inner):
            u = temp[n][s][p, k]
            coef[n][s][p, k] = kap[p, k] * recip(1.0 + u * u)

    def forward(s, n):
        u_ref, a_ref, new = temp[n][s], coef[n][s], temp[n + 1][s]

        def do(p):
            u0, a0 = u_ref[p, 0], a_ref[p, 0]
            ub, ab = wrapped(u_ref[p, inner - 1], 1, 0), wrapped(a_ref[p, inner - 1], 1, 0)
            low = (ab + a0) * (u0 - ub)
            u, a = u0, a0
            for k in range(inner):
                if k + 1 < inner:
                    uy, ay = u_ref[p, k + 1], a_ref[p, k + 1]
                else:
                    uy, ay = wrapped(u0, BLOCKS - 1, BLOCKS - 1), wrapped(a0, BLOCKS - 1, BLOCKS - 1)
                high = (a + ay) * (uy - u)
                flux = (a + a_ref[p + 1, k]) * (u_ref[p + 1, k] - u)
                flux = flux + (a + a_ref[p - 1, k]) * (u_ref[p - 1, k] - u)
                flux = flux + (high - low)
                flux = flux + (hz[s][p - 1, k] - jnp.where(first_lane, a * u, hz_low[s][p - 1, k]))
                later = (u + heat[s * STEPS + n, k]) + flux
                new[p, k] = later
                if n + 1 < STEPS:
                    coef[n + 1][s][p, k] = kap[p, k] * recip(1.0 + later * later)
                low, u, a = high, uy, ay

        return do

    def backward(s, n):
        whole = n > 0
        u_ref, a_ref = temp[n][s], coef[n][s]
        v_ref, new = lam[(n + 1) % 2][s], lam[n % 2][s]

        def do(p):
            def across(ref, k):
                if k < 0:
                    return wrapped(ref[p, inner - 1], 1, 0)
                if k == inner:
                    return wrapped(ref[p, 0], BLOCKS - 1, BLOCKS - 1)
                return ref[p, k]

            u, v = u_ref[p, 0], v_ref[p, 0]
            d = v - across(v_ref, -1)
            m_low = (u - across(u_ref, -1)) * d
            if whole:
                a = a_ref[p, 0]
                h_low = (a + across(a_ref, -1)) * d
            for k in range(inner):
                uy, vy = across(u_ref, k + 1), across(v_ref, k + 1)
                d = vy - v
                d_up, d_down = v_ref[p + 1, k] - v, v_ref[p - 1, k] - v
                m_high = (uy - u) * d
                total = (u_ref[p + 1, k] - u) * d_up + (u_ref[p - 1, k] - u) * d_down
                total = total + (m_high + m_low)
                total = total + (mz[s][p - 1, k] + jnp.where(first_lane, u * v, mz_low[s][p - 1, k]))
                t = total * recip(1.0 + u * u)
                acc[p - 1, k] = acc[p - 1, k] + t
                if whole:
                    ay = across(a_ref, k + 1)
                    h_high = (a + ay) * d
                    flux = (a + a_ref[p + 1, k]) * d_up + (a + a_ref[p - 1, k]) * d_down
                    flux = flux + (h_high - h_low)
                    flux = flux + (hz[s][p - 1, k] - jnp.where(first_lane, a * v, hz_low[s][p - 1, k]))
                    half = (a * u) * t
                    new[p, k] = (v + flux) + (half + half)
                    a, h_low = ay, h_high
                u, v, m_low = uy, vy, m_high

        return do

    def plane_of(t):
        away = jnp.where(top, t, planes + 1 - t)
        return jnp.where(t == 0, edge[0], away)

    def sweep(main, other, at):
        def body(t, c):
            for when, do in at.items():
                pl.when(t == when)(do)
            p = plane_of(t)
            past = plane_of(jnp.maximum(t - 1, 0))

            if other is not None:
                for part, q in ((other[1], past), (other[0], p)):
                    for k in range(inner):
                        part(q, k)
            if main is not None:
                main(p)
            return c

        lax.fori_loop(0, planes, body, 0)
        if other is not None:
            for k in range(inner):
                other[1](plane_of(planes - 1), k)

    def first_coef(p, c):
        for s in range(2):
            plane_coef(s, 0, p)
        return c

    lax.fori_loop(1, planes + 1, first_coef, 0)
    sweep(None, spread_temp(0, 0), {})

    def both_kap(side):
        each_side(side, lambda: move_kap(side).wait_recv())
        scale(halo[side])

    both_kap(1)
    both_kap(0)

    for n in range(STEPS):
        for s in range(2):

            def at_first(s=s, n=n):
                each_side(0, lambda: move_temp(0, s, n).wait_recv())
                plane_coef(s, n, halo[0])

            def at_second(s=s, n=n):
                if n + 1 < STEPS:
                    each_side(0, lambda: move_temp(0, s, n + 1).start())
                move_temp(1, s, n).wait_recv()
                plane_coef(s, n, halo[1])

            at = {0: at_first, 1: at_second}
            if n + 1 < STEPS:
                at[2] = lambda s=s, n=n: move_temp(1, s, n + 1).start()
            if s == 0:
                other = spread_temp(1, n)
            elif n + 1 < STEPS:
                other = spread_temp(0, n + 1)
            else:
                other = spread_lam(0, n, True)
            sweep(forward(s, n), other, at)
        if n == STEPS - 2:
            for s in range(2):
                for copy in loads[3 + s]:
                    copy.wait()
                for side in range(2):
                    each_side(side, lambda: move_lam(side, s, STEPS).start())

    stores = []
    for s in range(2):
        for b in range(BLOCKS):
            copy = pltpu.make_async_copy(
                temp[STEPS][s].at[pl.ds(1, planes), :, b, :],
                final_hbm.at[s, :, pl.ds(b * inner, inner), :],
                out_sem.at[s, b],
            )
            copy.start()
            stores.append(copy)

    for n in reversed(range(STEPS)):
        for s in range(2):

            def at_first(s=s, n=n):
                each_side(0, lambda: move_lam(0, s, n + 1).wait_recv())
                if 0 < n <= STEPS - 2:
                    each_side(0, lambda: move_lam(0, s, n + 2).wait_send())
                    move_lam(1, s, n + 2).wait_send()

            def at_second(s=s, n=n):
                if n > 0:
                    each_side(0, lambda: move_lam(0, s, n).start())
                move_lam(1, s, n + 1).wait_recv()

            at = {0: at_first, 1: at_second}
            if n > 0:
                at[2] = lambda s=s, n=n: move_lam(1, s, n).start()
            if s == 0:
                other = spread_lam(1, n, n > 0)
            elif n > 0:
                other = spread_lam(0, n - 1, n > 1)
            else:
                other = None
            sweep(backward(s, n), other, at)

    half = planes // 2
    shares = [
        pltpu.make_async_copy(acc.at[:, :, b, :], share.at[b // 4, b % 4], g_sem.at[b])
        for b in range(BLOCKS)
    ]
    for copy in shares:
        copy.start()
    for copy in shares:
        copy.wait()

    def along_x(way, slot, column, low):
        return pltpu.make_async_remote_copy(
            src_ref=share.at[:, column, pl.ds(low, half)],
            dst_ref=inbox.at[way, slot],
            send_sem=x_send.at[way, slot],
            recv_sem=x_recv.at[way, slot],
            device_id=(space, set_left if way else set_right),
            device_id_type=MESH,
        )

    column = (x_right, x_left)
    first = (0, half)
    sends = [along_x(way, 0, x_far, first[way]) for way in range(2)]
    sends += [along_x(way, 1, column[way], half - first[way]) for way in range(2)]
    for copy in sends:
        copy.start()

    def add_in(y, column, low, way, slot):
        for p in range(half):
            share[y, column, low + p] = share[y, column, low + p] + inbox[way, slot, y, p]

    for way in range(2):
        sends[way].wait_recv()
        for y in range(2):
            add_in(y, column[way], first[way], way, 0)
        onward = along_x(way, 2, column[way], first[way])
        onward.start()
        sends.append(onward)
    for way in range(2):
        along_x(way, 1, column[way], half - first[way]).wait_recv()
        for y in range(2):
            add_in(y, own_x, half - first[way], way, 1)

    def along_y(way):
        return pltpu.make_async_remote_copy(
            src_ref=share.at[1 - own_y, own_x, pl.ds(first[way], half)],
            dst_ref=inbox_y.at[pl.ds(first[way], half)],
            send_sem=y_send.at[way],
            recv_sem=y_recv.at[way],
            device_id=(space, set_y),
            device_id_type=MESH,
        )

    for way in range(2):
        along_x(way, 2, column[way], first[way]).wait_recv()
        add_in(1 - own_y, own_x, first[way], way, 2)
        along_y(way).start()
        add_in(own_y, own_x, first[way], way, 2)
    for way in range(2):
        along_y(way).wait_recv()
        for p in range(half):
            q = first[way] + p
            inbox_y[q] = -HALF * (share[own_y, own_x, q] + inbox_y[q])
        copy = pltpu.make_async_copy(
            inbox_y.at[pl.ds(first[way], half)], grad_hbm.at[pl.ds(first[way], half)], out_sem.at[2, way]
        )
        copy.start()
        stores.append(copy)
    for copy in sends:
        copy.wait_send()
    for way in range(2):
        along_y(way).wait_send()
    for s in range(2):
        for n in range(STEPS):
            each_side(0, lambda: move_temp(0, s, n).wait_send())
            move_temp(1, s, n).wait_send()
        for m in (1, 2):
            each_side(0, lambda: move_lam(0, s, m).wait_send())
            move_lam(1, s, m).wait_send()
    for copy in stores:
        copy.wait()


def local(set_size, space_size, initial, conductivity, weights, setting_index, track, power):
    settings, planes, y_count, lanes = initial.shape
    inner = y_count // BLOCKS
    tile = (inner, BLOCKS, lanes)
    any_ref = pl.BlockSpec(memory_space=pl.ANY)
    smem = pl.BlockSpec(memory_space=pltpu.SMEM)
    f32 = jnp.float32
    dma = pltpu.SemaphoreType.DMA
    return pl.pallas_call(
        functools.partial(kernel, planes, inner, set_size, space_size),
        out_shape=(
            jax.ShapeDtypeStruct(initial.shape, f32),
            jax.ShapeDtypeStruct((planes, y_count // set_size, lanes), f32),
        ),
        in_specs=[any_ref] * 3 + [smem] * 3,
        out_specs=[any_ref] * 2,
        scratch_shapes=[pltpu.VMEM((planes + 2,) + tile, f32)] * (4 * STEPS + 2)
        + [pltpu.VMEM((planes,) + tile, f32)] * (4 * STEPS)
        + [pltpu.VMEM((planes + 2,) + tile, f32)] * 4
        + [pltpu.VMEM((planes,) + tile, f32)] * 8
        + [
            pltpu.VMEM((planes + 2,) + tile, f32),
            pltpu.VMEM((settings * STEPS,) + tile, f32),
            pltpu.VMEM((planes,) + tile, f32),
            pltpu.VMEM(tile, f32),
            pltpu.VMEM(tile, f32),
            pltpu.VMEM((2, 4, planes, inner, lanes), f32),
            pltpu.VMEM((2, 3, 2, planes // 2, inner, lanes), f32),
            pltpu.VMEM((planes, inner, lanes), f32),
            dma((5, BLOCKS)),
            dma((3, BLOCKS)),
            dma((2,)),
            dma((2,)),
            dma((2, settings, STEPS)),
            dma((2, settings, STEPS)),
            dma((2, settings, STEPS + 1)),
            dma((2, settings, STEPS + 1)),
            dma((BLOCKS,)),
            dma((2, 3)),
            dma((2, 3)),
            dma((2,)),
            dma((2,)),
        ],
        compiler_params=pltpu.CompilerParams(
            collective_id=0, has_side_effects=True, vmem_limit_bytes=62 * 2**20
        ),
    )(initial, conductivity, weights, setting_index, track, power)


def solution(mesh):
    in_specs = (
        P("set", "space", None, None),
        P("space", None, None),
        P("set", "space", None, None),
        P("set"),
        P(),
        P(),
    )
    out_specs = (P("set", "space", None, None), P("space", "set", None))
    return jax.shard_map(
        functools.partial(local, mesh.shape["set"], mesh.shape["space"]),
        mesh=mesh,
        in_specs=in_specs,
        out_specs=out_specs,
        check_vma=False,
    )
```

time: 304 us -> 72.6 us (0.24)
  other arithmetic: 124 us -> 0 us
  waiting for transfers between devices: 98.1 us -> 0 us
  Pallas kernels: 0 us -> 65 us
  starting transfers between devices: 57 us -> 0 us
  between operations: 14.5 us -> 0.65 us
    pallas_call x0 -> x1, Pallas kernels: none -> 65 us  [local(): pl.pallas_call(functools.partial(kernel, planes, inner, set_size, space_s...]
    reduce_scatter x1 -> x0, waiting for transfers between devices: 63 us -> none  [local(): owned = lax.psum_scatter(gradient, 'set', scatter_dimension=1, tiled=True)]
    ppermute x16 -> x0, starting transfers between devices: 56.9 us -> none  [the longest x8 40.3 us: with_halo(): after = lax.ppermute(initial, axis, down)]
    add x5 -> x0, other arithmetic: 49.2 us -> none  [the longest x3 36.1 us: local(): adjoint = grad_temp + grad_coef * kappa * conduct_slope(centre_temp)]
    reduce_sum x5 -> x0, other arithmetic: 37.9 us -> none  [the longest x4 37.8 us: local(): gradient = gradient + jnp.sum(grad_coef * conduct(centre_temp), axis=0)]
    ppermute x16 -> x0, waiting for transfers between devices: 35.1 us -> none  [the longest x8 23.4 us: with_halo(): before = lax.ppermute(last, axis, up)]
    concatenate x8 -> x0, other arithmetic: 19.5 us -> none  [with_halo(): shard = jnp.concatenate([before, shard, after], axis=dim)]
    another operation x4 -> x0, other arithmetic: 14.7 us -> none  [local(): stacked = with_halo(jnp.stack((thermal, coeffs)), (('space', 2),), 1)]
  transfers between devices with their start and end apart: 17 -> 0, of which waited for: 14 -> 0; matrix products, arithmetic and copies ran while one was open for 8% -> 0% of each run, Pallas kernels for 0% -> 0%
where the time goes in v1:
time: 72.6 us; the launch traced here: 72.2 us
  Pallas kernels  65 us (90%)
  local copies, waits for them, and re-layouts  6.58 us (9%)
    pallas_call x1, Pallas kernels, local(): pl.pallas_call(functools.partial(kernel, planes, inner, set_size, space_s...  65 us
    unnamed x6, local copies, waits for them, and re-layouts  6.58 us

profile of v1, /device:TPU:8, one launch (start us, length us, event | category | flops | bytes accessed | tf_op | source)
XLA Modules:
  0.0 72.2 jit_solution(1773652854276746686)
XLA Ops:
  0.6 1.4 %copy.8.refs_4_ = s32[64,4]{1,0:T(8,128)} copy(s32[64,4]{0,1:T(4,128)} %param.10) | data formatting | bytes 2048 | tf_op args[4]
  2.0 1.4 %copy.9.refs_5_ = s32[64,4]{1,0:T(8,128)} copy(s32[64,4]{0,1:T(4,128)} %param.11) | data formatting | bytes 2048 | tf_op args[5]
  3.4 65.0 %shard_map.77 = (f32[2,8,256,128]{3,2,1,0:T(8,128)}, f32[8,32,128]{2,1,0:T(8,128)}) custom-call(f32[2,8,256,128]{3,2,1,0:T(8,128)} %refs_0_.1, f32[8,256,128]{2,1,0:T(8,128)} %refs_1_.1, f32[2,8,256,128]{3,2,1,0:T(8,128)} %refs_2_.1, s32[2]{0:T(128)} %refs_3_.1, s32[64,4]{1,0:T(8,128)} %copy.8.refs_4_, s32[64,4]{1,0:T(8,128)} %copy.9.refs_5_), custom_call_target="tpu_custom_call" | custom-call | tf_op jit(solution)/shard_map/pallas_call | solution.py:494
  68.4 0.0 copy-start
  68.4 3.1 %copy.12 = f32[2,8,256,128]{3,2,1,0:T(8,128)} copy(f32[2,8,256,128]{3,2,1,0:T(8,128)} %get-tuple-element.4) | data formatting | bytes 4194304
  71.6 0.0 copy-done
  71.6 0.7 copy.13
Async XLA Ops:
  68.4 3.2 %copy-start = (f32[8,32,128]{2,1,0:T(8,128)S(1)}, f32[8,32,128]{2,1,0:T(8,128)}, u32[]{:S(2)}) copy-start(f32[8,32,128]{2,1,0:T(8,128)} %get-tuple-element.5) | copy-start | bytes 393220

commit v2 on v1

v2 whole, which is shorter than its diff:
```python
import functools

import jax
import jax.numpy as jnp
from jax import lax
from jax.experimental import pallas as pl
from jax.experimental.pallas import tpu as pltpu
from jax.sharding import PartitionSpec as P

STEPS = 4
DT = 0.15
HALF = 0.5 * DT
BLOCKS = 8
LANES = 128
MESH = pl.DeviceIdType.MESH


def recip(value):
    return pl.reciprocal(value, approx=True)


def kernel(planes, inner, set_size, space_size, *refs):
    init_hbm, cond_hbm, weights_hbm, index_smem, track_smem, power_smem, final_hbm, grad_hbm = refs[:8]
    refs = list(refs[8:])

    def take(*shape):
        if not shape:
            return refs.pop(0)
        return [take(*shape[1:]) for _ in range(shape[0])]

    temp = take(STEPS + 1, 2)
    coef = take(STEPS, 2)
    az = take(STEPS, 2)
    dz = take(STEPS, 2)
    lam = take(2, 2)
    hz, hz_low, mz, mz_low = (take(2) for _ in range(4))
    kap, heat, acc, roll_u, roll_a = (take() for _ in range(5))
    share, inbox, inbox_y = (take() for _ in range(3))
    in_sem, out_sem, k_send, k_recv, u_send, u_recv, l_send, l_recv, g_sem, x_send, x_recv, y_send, y_recv = (
        take() for _ in range(13)
    )
    space = lax.axis_index("space")
    own_set = lax.axis_index("set")
    core = lax.rem(space, 2)
    top = core == 1
    edge = (jnp.where(top, planes, 1), jnp.where(top, 1, planes))
    halo = (jnp.where(top, planes + 1, 0), jnp.where(top, 0, planes + 1))
    there = (jnp.where(top, 0, planes + 1), jnp.where(top, planes + 1, 0))
    partner = (
        jnp.clip(jnp.where(top, space + 1, space - 1), 0, space_size - 1),
        jnp.where(top, space - 1, space + 1),
    )
    has_far = jnp.logical_and(space != 0, space != space_size - 1)
    lane = lax.broadcasted_iota(jnp.int32, (BLOCKS, LANES), 1)
    sub = lax.broadcasted_iota(jnp.int32, (BLOCKS, LANES), 0)
    not_last = lane < LANES - 1
    first_lane = lane == 0

    def relayout(src, dst, sem):
        return [
            pltpu.make_async_copy(
                src.at[:, pl.ds(b * inner, inner), :],
                dst.at[pl.ds(1, planes), :, b, :],
                sem.at[b],
            )
            for b in range(BLOCKS)
        ]

    loads = [
        relayout(init_hbm.at[0], temp[0][0], in_sem.at[0]),
        relayout(cond_hbm, kap, in_sem.at[1]),
        relayout(init_hbm.at[1], temp[0][1], in_sem.at[2]),
        relayout(weights_hbm.at[0], lam[0][0], in_sem.at[3]),
        relayout(weights_hbm.at[1], lam[0][1], in_sem.at[4]),
    ]
    for group in loads:
        for copy in group:
            copy.start()

    barrier = pltpu.get_barrier_semaphore()
    pl.semaphore_signal(barrier, inc=1, device_id=(partner[1], own_set), device_id_type=MESH)

    @pl.when(has_far)
    def _():
        pl.semaphore_signal(barrier, inc=1, device_id=(partner[0], own_set), device_id_type=MESH)

    own_y, own_x = own_set // 4, lax.rem(own_set, 4)
    x_right, x_left, x_far = (lax.rem(own_x + i, 4) for i in (1, 3, 2))
    set_right, set_left = own_y * 4 + x_right, own_y * 4 + x_left
    set_y = (1 - own_y) * 4 + own_x
    for other_set in (set_right, set_left, set_y):
        pl.semaphore_signal(barrier, inc=1, device_id=(space, other_set), device_id_type=MESH)

    part = inner // 2

    def swap(ref, lane_id, send, recv):
        side = lane_id // 2
        rows = pl.ds(0, inner) if side else pl.ds(lane_id * part, part)
        return pltpu.make_async_remote_copy(
            src_ref=ref.at[edge[side], rows],
            dst_ref=ref.at[there[side], rows],
            send_sem=send,
            recv_sem=recv,
            device_id=(partner[side], own_set),
            device_id_type=MESH,
        )

    def move_temp(i, s, n):
        return swap(temp[n][s], i, u_send.at[i, s, n], u_recv.at[i, s, n])

    def move_lam(i, s, m):
        return swap(lam[m % 2][s], i, l_send.at[i, s, m], l_recv.at[i, s, m])

    def move_kap(i):
        return swap(kap, i, k_send.at[i], k_recv.at[i])

    def each_way(i, do):
        if i == 2:
            do()
        else:
            pl.when(has_far)(do)

    @pl.when(jnp.logical_not(has_far))
    def _():
        zero = jnp.zeros((inner, BLOCKS, LANES), jnp.float32)
        kap[halo[0]] = zero
        for s in range(2):
            for n in range(STEPS):
                temp[n][s][halo[0]] = zero
            for n in range(2):
                lam[n][s][halo[0]] = zero

    prof_z = jnp.exp(-4.0 * lane.astype(jnp.float32) / LANES)

    def make_heat(i, carry):
        s = i // STEPS
        n = lax.rem(i, STEPS)
        row = index_smem[s]
        y0 = track_smem[n, row].astype(jnp.float32)
        level = power_smem[n, row].astype(jnp.float32)
        plane = prof_z * (DT * 0.5 * (1.0 + level))

        def rows(y, c):
            offset = ((sub * inner + y).astype(jnp.float32) - y0) * (16.0 / (inner * BLOCKS))
            heat[i, y] = plane * jnp.exp(-(offset * offset))
            return c

        return lax.fori_loop(0, inner, rows, carry, unroll=8)

    lax.fori_loop(0, 2 * STEPS, make_heat, 0)

    def clear(y, c):
        for p in range(planes):
            acc[p, y] = jnp.zeros((BLOCKS, LANES), jnp.float32)
        return c

    lax.fori_loop(0, inner, clear, 0)

    pl.semaphore_wait(barrier, jnp.where(has_far, 5, 4))

    for which, go in ((0, lambda i: move_temp(i, 0, 0)), (1, move_kap), (2, lambda i: move_temp(i, 1, 0))):
        for copy in loads[which]:
            copy.wait()
        for i in range(3):
            each_way(i, lambda go=go, i=i: go(i).start())

    def scale(p):
        for k in range(inner):
            kap[p, k] = HALF * kap[p, k]

    for i in range(3):
        each_way(i, lambda i=i: move_kap(i).wait_send())

    def scale_all(p, c):
        scale(p)
        return c

    lax.fori_loop(1, planes + 1, scale_all, 0)

    def wrapped(value, shift, last):
        return jnp.where(sub == last, 0.0, pltpu.roll(value, shift, 0))

    def across(ref, p, k):
        if k < 0:
            return wrapped(ref[p, inner - 1], 1, 0)
        if k == inner:
            return wrapped(ref[p, 0], BLOCKS - 1, BLOCKS - 1)
        return ref[p, k]

    def shifted(value):
        return pltpu.roll(value, LANES - 1, 1)

    def spread_temp(s, n):
        u_ref, a_ref = temp[n][s], coef[n][s]

        def first(p, k):
            roll_u[k] = shifted(u_ref[p, k])
            roll_a[k] = shifted(a_ref[p, k])

        def second(p, k):
            u, a = u_ref[p, k], a_ref[p, k]
            face = a + jnp.where(not_last, roll_a[k], 0.0)
            diff = jnp.where(not_last, roll_u[k], 0.0) - u
            g = face * diff
            az[n][s][p - 1, k] = face
            dz[n][s][p - 1, k] = diff
            hz[s][p - 1, k] = g
            hz_low[s][p - 1, k] = pltpu.roll(g, 1, 1)

        return first, second

    def spread_lam(s, n, whole):
        v_ref = lam[(n + 1) % 2][s]

        def first(p, k):
            roll_u[k] = shifted(v_ref[p, k])

        def second(p, k):
            d = jnp.where(not_last, roll_u[k], 0.0) - v_ref[p, k]
            m = dz[n][s][p - 1, k] * d
            mz[s][p - 1, k] = m
            mz_low[s][p - 1, k] = pltpu.roll(m, 1, 1)
            if whole:
                h = az[n][s][p - 1, k] * d
                hz[s][p - 1, k] = h
                hz_low[s][p - 1, k] = pltpu.roll(h, 1, 1)

        return first, second

    def plane_coef(s, n, p, rows=range(inner)):
        for k in rows:
            u = temp[n][s][p, k]
            coef[n][s][p, k] = kap[p, k] * recip(1.0 + u * u)

    def forward(s, n):
        u_ref, a_ref, new = temp[n][s], coef[n][s], temp[n + 1][s]

        def do(p, rows=range(inner)):
            u, a = u_ref[p, rows[0]], a_ref[p, rows[0]]
            low = (across(a_ref, p, rows[0] - 1) + a) * (u - across(u_ref, p, rows[0] - 1))
            for k in rows:
                uy, ay = across(u_ref, p, k + 1), across(a_ref, p, k + 1)
                high = (a + ay) * (uy - u)
                flux = (a + a_ref[p + 1, k]) * (u_ref[p + 1, k] - u)
                flux = flux + (a + a_ref[p - 1, k]) * (u_ref[p - 1, k] - u)
                flux = flux + (high - low)
                flux = flux + (hz[s][p - 1, k] - jnp.where(first_lane, a * u, hz_low[s][p - 1, k]))
                later = (u + heat[s * STEPS + n, k]) + flux
                new[p, k] = later
                if n + 1 < STEPS:
                    coef[n + 1][s][p, k] = kap[p, k] * recip(1.0 + later * later)
                low, u, a = high, uy, ay

        return do

    def backward(s, n):
        whole = n > 0
        u_ref, a_ref = temp[n][s], coef[n][s]
        v_ref, new = lam[(n + 1) % 2][s], lam[n % 2][s]

        def do(p, rows=range(inner)):
            u, v = u_ref[p, rows[0]], v_ref[p, rows[0]]
            d = v - across(v_ref, p, rows[0] - 1)
            m_low = (u - across(u_ref, p, rows[0] - 1)) * d
            if whole:
                a = a_ref[p, rows[0]]
                h_low = (a + across(a_ref, p, rows[0] - 1)) * d
            for k in rows:
                uy, vy = across(u_ref, p, k + 1), across(v_ref, p, k + 1)
                d = vy - v
                d_up, d_down = v_ref[p + 1, k] - v, v_ref[p - 1, k] - v
                m_high = (uy - u) * d
                total = (u_ref[p + 1, k] - u) * d_up + (u_ref[p - 1, k] - u) * d_down
                total = total + (m_high + m_low)
                total = total + (mz[s][p - 1, k] + jnp.where(first_lane, u * v, mz_low[s][p - 1, k]))
                t = total * recip(1.0 + u * u)
                acc[p - 1, k] = acc[p - 1, k] + t
                if whole:
                    ay = across(a_ref, p, k + 1)
                    h_high = (a + ay) * d
                    flux = (a + a_ref[p + 1, k]) * d_up + (a + a_ref[p - 1, k]) * d_down
                    flux = flux + (h_high - h_low)
                    flux = flux + (hz[s][p - 1, k] - jnp.where(first_lane, a * v, hz_low[s][p - 1, k]))
                    half = (a * u) * t
                    new[p, k] = (v + flux) + (half + half)
                    a, h_low = ay, h_high
                u, v, m_low = uy, vy, m_high

        return do

    def plane_of(t):
        away = jnp.where(top, t, planes + 1 - t)
        return jnp.where(t == 0, edge[0], away)

    def sweep(main, other, ahead, behind, at):
        for h in range(2):
            rows = range(h * part, (h + 1) * part)
            ahead(h)
            for k in rows:
                other[0](edge[0], k)
            main(edge[0], rows)
            behind(h)

        def body(t, c):
            for when, do in at.items():
                pl.when(t == when)(do)
            for one, q in ((other[1], plane_of(t - 1)), (other[0], plane_of(t))):
                for k in range(inner):
                    one(q, k)
            main(plane_of(t))
            return c

        lax.fori_loop(1, planes, body, 0)
        for k in range(inner):
            other[1](plane_of(planes - 1), k)

    def first_coef(p, c):
        for s in range(2):
            plane_coef(s, 0, p)
        return c

    lax.fori_loop(1, planes + 1, first_coef, 0)
    begin = spread_temp(0, 0)

    def begin_z(t, c):
        for one, q in ((begin[1], jnp.maximum(t, 1)), (begin[0], t + 1)):
            for k in range(inner):
                one(q, k)
        return c

    lax.fori_loop(0, planes, begin_z, 0)
    for k in range(inner):
        begin[1](planes, k)
    for i in range(3):
        each_way(i, lambda i=i: move_kap(i).wait_recv())
    for side in range(2):
        scale(halo[side])

    for n in range(STEPS):
        for s in range(2):

            def ahead(h, s=s, n=n):
                each_way(0, lambda: move_temp(h, s, n).wait_recv())
                plane_coef(s, n, halo[0], range(h * part, (h + 1) * part))

            def behind(h, s=s, n=n):
                if n + 1 < STEPS:
                    each_way(h, lambda: move_temp(h, s, n + 1).start())

            def near(s=s, n=n):
                move_temp(2, s, n).wait_recv()
                plane_coef(s, n, halo[1])

            at = {1: near}
            if n + 1 < STEPS:
                at[2] = lambda s=s, n=n: move_temp(2, s, n + 1).start()
            if s == 0:
                other = spread_temp(1, n)
            elif n + 1 < STEPS:
                other = spread_temp(0, n + 1)
            else:
                other = spread_lam(0, n, True)
            sweep(forward(s, n), other, ahead, behind, at)
        if n == STEPS - 2:
            for s in range(2):
                for copy in loads[3 + s]:
                    copy.wait()
                for i in range(3):
                    each_way(i, lambda i=i: move_lam(i, s, STEPS).start())

    stores = []
    for s in range(2):
        for b in range(BLOCKS):
            copy = pltpu.make_async_copy(
                temp[STEPS][s].at[pl.ds(1, planes), :, b, :],
                final_hbm.at[s, :, pl.ds(b * inner, inner), :],
                out_sem.at[s, b],
            )
            copy.start()
            stores.append(copy)

    for n in reversed(range(STEPS)):
        for s in range(2 if n > 0 else 1):

            def ahead(h, s=s, n=n):
                each_way(h, lambda: move_lam(h, s, n + 1).wait_recv())
                if h == 0 and 0 < n <= STEPS - 2:
                    for i in range(3):
                        each_way(i, lambda i=i: move_lam(i, s, n + 2).wait_send())

            def behind(h, s=s, n=n):
                if n > 0:
                    each_way(h, lambda: move_lam(h, s, n).start())

            at = {1: lambda s=s, n=n: move_lam(2, s, n + 1).wait_recv()}
            if n > 0:
                at[2] = lambda s=s, n=n: move_lam(2, s, n).start()
            if s == 0:
                other = spread_lam(1, n, n > 0)
            else:
                other = spread_lam(0, n - 1, n > 1)
            sweep(backward(s, n), other, ahead, behind, at)

    def row_of(t):
        return plane_of(t + 1) - 1

    def shares(t):
        q = row_of(t)
        return [
            pltpu.make_async_copy(acc.at[q, :, b, :], share.at[b // 4, b % 4, q], g_sem.at[t, b])
            for b in range(BLOCKS)
        ]

    def along_x(t, slot):
        right = (lax.rem(t, 2) == 0) if slot != 1 else (lax.rem(t, 2) == 1)
        column = x_far if slot == 0 else jnp.where(right, x_right, x_left)
        return pltpu.make_async_remote_copy(
            src_ref=share.at[:, column, row_of(t)],
            dst_ref=inbox.at[slot, t],
            send_sem=x_send.at[slot, t],
            recv_sem=x_recv.at[slot, t],
            device_id=(space, jnp.where(right, set_right, set_left)),
            device_id_type=MESH,
        )

    def along_y(t):
        q = row_of(t)
        return pltpu.make_async_remote_copy(
            src_ref=share.at[1 - own_y, own_x, q],
            dst_ref=inbox_y.at[q],
            send_sem=y_send.at[t],
            recv_sem=y_recv.at[t],
            device_id=(space, set_y),
            device_id_type=MESH,
        )

    def start_shares(t):
        for copy in shares(t):
            copy.start()

    def send_shares(t):
        for copy in shares(t):
            copy.wait()
        along_x(t, 0).start()

    def last_body(t, c):
        @pl.when(t == 0)
        def _():
            move_lam(2, 1, 1).wait_recv()

        @pl.when(t == planes - 1)
        def _():
            for h in range(2):
                each_way(h, lambda h=h: move_lam(h, 1, 1).wait_recv())

        pl.when(t >= 1)(lambda: start_shares(t - 1))
        pl.when(t >= 2)(lambda: send_shares(t - 2))
        backward(1, 0)(plane_of(t + 1))
        return c

    lax.fori_loop(0, planes, last_body, 0)
    start_shares(planes - 1)
    send_shares(planes - 2)
    send_shares(planes - 1)

    def pass_on(t, c):
        along_x(t, 0).wait_recv()
        q = row_of(t)
        column = jnp.where(lax.rem(t, 2) == 0, x_right, x_left)
        for y in range(2):
            share[y, column, q] = share[y, column, q] + inbox[0, t, y]
        along_x(t, 2).start()
        along_x(t, 1).start()
        return c

    lax.fori_loop(0, planes, pass_on, 0)

    def across_y(t, c):
        along_x(t, 1).wait_recv()
        along_x(t, 2).wait_recv()
        q = row_of(t)
        for y in (1 - own_y, own_y):
            share[y, own_x, q] = share[y, own_x, q] + (inbox[1, t, y] + inbox[2, t, y])
        along_y(t).start()
        return c

    lax.fori_loop(0, planes, across_y, 0)

    def give(t):
        q = row_of(t)
        return pltpu.make_async_copy(inbox_y.at[q], grad_hbm.at[q], out_sem.at[2, t])

    def last_add(t, c):
        along_y(t).wait_recv()
        q = row_of(t)
        inbox_y[q] = -HALF * (share[own_y, own_x, q] + inbox_y[q])
        give(t).start()
        return c

    lax.fori_loop(0, planes, last_add, 0)

    def drain(t, c):
        for slot in range(3):
            along_x(t, slot).wait_send()
        along_y(t).wait_send()
        give(t).wait()
        return c

    lax.fori_loop(0, planes, drain, 0)
    for s in range(2):
        for i in range(3):
            for n in range(STEPS):
                each_way(i, lambda s=s, i=i, n=n: move_temp(i, s, n).wait_send())
            for m in (1, 2):
                each_way(i, lambda s=s, i=i, m=m: move_lam(i, s, m).wait_send())
    for copy in stores:
        copy.wait()


def hand_over(final, gradient, final_out, gradient_out, held, held_grad, sems):
    spots = [(s, p) for s in range(final.shape[0]) for p in range(final.shape[1])]
    moves = [(gradient, held_grad, gradient_out)]
    moves += [(final.at[s, p], held.at[s, p], final_out.at[s, p]) for s, p in spots]
    loads = [pltpu.make_async_copy(a, b, sems.at[0, i]) for i, (a, b, _) in enumerate(moves)]
    stores = [pltpu.make_async_copy(b, c, sems.at[1, i]) for i, (_, b, c) in enumerate(moves)]
    for copy in loads:
        copy.start()
    for load, store in zip(loads, stores):
        load.wait()
        store.start()
    for store in stores:
        store.wait()


def local(set_size, space_size, initial, conductivity, weights, setting_index, track, power):
    settings, planes, y_count, lanes = initial.shape
    inner = y_count // BLOCKS
    tile = (inner, BLOCKS, lanes)
    any_ref = pl.BlockSpec(memory_space=pl.ANY)
    smem = pl.BlockSpec(memory_space=pltpu.SMEM)
    f32 = jnp.float32
    dma = pltpu.SemaphoreType.DMA
    final, gradient = pl.pallas_call(
        functools.partial(kernel, planes, inner, set_size, space_size),
        out_shape=(
            jax.ShapeDtypeStruct(initial.shape, f32),
            jax.ShapeDtypeStruct((planes, y_count // set_size, lanes), f32),
        ),
        in_specs=[any_ref] * 3 + [smem] * 3,
        out_specs=[any_ref] * 2,
        scratch_shapes=[pltpu.VMEM((planes + 2,) + tile, f32)] * (4 * STEPS + 2)
        + [pltpu.VMEM((planes,) + tile, f32)] * (4 * STEPS)
        + [pltpu.VMEM((planes + 2,) + tile, f32)] * 4
        + [pltpu.VMEM((planes,) + tile, f32)] * 8
        + [
            pltpu.VMEM((planes + 2,) + tile, f32),
            pltpu.VMEM((settings * STEPS,) + tile, f32),
            pltpu.VMEM((planes,) + tile, f32),
            pltpu.VMEM(tile, f32),
            pltpu.VMEM(tile, f32),
            pltpu.VMEM((2, 4, planes, inner, lanes), f32),
            pltpu.VMEM((3, planes, 2, inner, lanes), f32),
            pltpu.VMEM((planes, inner, lanes), f32),
            dma((5, BLOCKS)),
            dma((3, BLOCKS)),
            dma((3,)),
            dma((3,)),
            dma((3, settings, STEPS)),
            dma((3, settings, STEPS)),
            dma((3, settings, STEPS + 1)),
            dma((3, settings, STEPS + 1)),
            dma((planes, BLOCKS)),
            dma((3, planes)),
            dma((3, planes)),
            dma((planes,)),
            dma((planes,)),
        ],
        compiler_params=pltpu.CompilerParams(
            collective_id=0, has_side_effects=True, vmem_limit_bytes=62 * 2**20
        ),
    )(initial, conductivity, weights, setting_index, track.T, power.T)
    return pl.pallas_call(
        hand_over,
        out_shape=(
            jax.ShapeDtypeStruct(final.shape, f32),
            jax.ShapeDtypeStruct(gradient.shape, f32),
        ),
        in_specs=[any_ref] * 2,
        out_specs=[any_ref] * 2,
        scratch_shapes=[
            pltpu.VMEM(final.shape, f32),
            pltpu.VMEM(gradient.shape, f32),
            dma((2, settings * planes + 1)),
        ],
    )(final, gradient)


def solution(mesh):
    in_specs = (
        P("set", "space", None, None),
        P("space", None, None),
        P("set", "space", None, None),
        P("set"),
        P(),
        P(),
    )
    out_specs = (P("set", "space", None, None), P("space", "set", None))
    return jax.shard_map(
        functools.partial(local, mesh.shape["set"], mesh.shape["space"]),
        mesh=mesh,
        in_specs=in_specs,
        out_specs=out_specs,
        check_vma=False,
    )
```

time: 72.6 us -> 64.7 us (0.89)
  local copies, waits for them, and re-layouts: 6.58 us -> 0 us
  Pallas kernels: 65 us -> 63.8 us
    unnamed x6 -> x0, local copies, waits for them, and re-layouts: 6.58 us -> none
    pallas_call x1, Pallas kernels: 65 us -> 61.2 us  [local(): pl.pallas_call(functools.partial(kernel, planes, inner, set_size, space_s...]
    pallas_call x0 -> x1, Pallas kernels: none -> 2.63 us  [local(): pl.pallas_call(hand_over, out_shape=(jax.ShapeDtypeStruct(final.shape, f3...]
where the time goes in v2:
time: 64.7 us; the launch traced here: 64.5 us
  Pallas kernels  63.8 us (99%)
    pallas_call x1, Pallas kernels, local(): pl.pallas_call(functools.partial(kernel, planes, inner, set_size, space_s...  61.2 us
    pallas_call x1, Pallas kernels, local(): pl.pallas_call(hand_over, out_shape=(jax.ShapeDtypeStruct(final.shape, f3...  2.63 us

profile of v2, /device:TPU:8, one launch (start us, length us, event | category | flops | bytes accessed | tf_op | source)
XLA Modules:
  0.0 64.5 jit_solution(14084696430348271855)
XLA Ops:
  0.6 61.2 %shard_map.77 = (f32[2,8,256,128]{3,2,1,0:T(8,128)}, f32[8,32,128]{2,1,0:T(8,128)}) custom-call(f32[2,8,256,128]{3,2,1,0:T(8,128)} %refs_0_.1, f32[8,256,128]{2,1,0:T(8,128)} %refs_1_.1, f32[2,8,256,128]{3,2,1,0:T(8,128)} %refs_2_.1, s32[2]{0:T(128)} %refs_3_.1, s32[4,64]{1,0:T(4,128)} %bitcast.2, s32[4,64]{1,0:T(4,128)} %bitcast.3), custom_call_target="tpu_custom_call" | custom-call | tf_op jit(solution)/shard_map/pallas_call | solution.py:543
  61.9 2.6 %shard_map.78 = (f32[2,8,256,128]{3,2,1,0:T(8,128)}, f32[8,32,128]{2,1,0:T(8,128)}) custom-call(f32[2,8,256,128]{3,2,1,0:T(8,128)} %get-tuple-element.4.final, f32[8,32,128]{2,1,0:T(8,128)} %get-tuple-element.5.gradient), custom_call_target="tpu_custom_call" | custom-call | tf_op jit(solution)/shard_map/pallas_call | solution.py:582

commit v3 on v2

--- a/solution.py
+++ b/solution.py
@@ -130,6 +130,18 @@
             for n in range(2):
                 lam[n][s][halo[0]] = zero
 
+    pl.semaphore_wait(barrier, jnp.where(has_far, 5, 4))
+
+    for which, go in ((0, lambda i: move_temp(i, 0, 0)), (1, move_kap), (2, lambda i: move_temp(i, 1, 0))):
+        for copy in loads[which]:
+            copy.wait()
+        for i in range(3):
+            each_way(i, lambda go=go, i=i: go(i).start())
+
+    def scale(p):
+        for k in range(inner):
+            kap[p, k] = HALF * kap[p, k]
+
     prof_z = jnp.exp(-4.0 * lane.astype(jnp.float32) / LANES)
 
     def make_heat(i, carry):
@@ -155,18 +167,6 @@
         return c
 
     lax.fori_loop(0, inner, clear, 0)
-
-    pl.semaphore_wait(barrier, jnp.where(has_far, 5, 4))
-
-    for which, go in ((0, lambda i: move_temp(i, 0, 0)), (1, move_kap), (2, lambda i: move_temp(i, 1, 0))):
-        for copy in loads[which]:
-            copy.wait()
-        for i in range(3):
-            each_way(i, lambda go=go, i=i: go(i).start())
-
-    def scale(p):
-        for k in range(inner):
-            kap[p, k] = HALF * kap[p, k]
 
     for i in range(3):
         each_way(i, lambda i=i: move_kap(i).wait_send())

time: 64.7 us -> 64.7 us (level)
  no operation moved by 1% of the time
where the time goes in v3:
time: 64.7 us; the launch traced here: 64.5 us
  Pallas kernels  63.8 us (99%)
    pallas_call x1, Pallas kernels, local(): pl.pallas_call(functools.partial(kernel, planes, inner, set_size, space_s...  61.2 us
    pallas_call x1, Pallas kernels, local(): pl.pallas_call(hand_over, out_shape=(jax.ShapeDtypeStruct(final.shape, f3...  2.63 us

profile of v3, /device:TPU:8, one launch (start us, length us, event | category | flops | bytes accessed | tf_op | source)
XLA Modules:
  0.0 64.5 jit_solution(6036029822991292413)
XLA Ops:
  0.6 61.2 %shard_map.77 = (f32[2,8,256,128]{3,2,1,0:T(8,128)}, f32[8,32,128]{2,1,0:T(8,128)}) custom-call(f32[2,8,256,128]{3,2,1,0:T(8,128)} %refs_0_.1, f32[8,256,128]{2,1,0:T(8,128)} %refs_1_.1, f32[2,8,256,128]{3,2,1,0:T(8,128)} %refs_2_.1, s32[2]{0:T(128)} %refs_3_.1, s32[4,64]{1,0:T(4,128)} %bitcast.2, s32[4,64]{1,0:T(4,128)} %bitcast.3), custom_call_target="tpu_custom_call" | custom-call | tf_op jit(solution)/shard_map/pallas_call | solution.py:543
  61.9 2.6 %shard_map.78 = (f32[2,8,256,128]{3,2,1,0:T(8,128)}, f32[8,32,128]{2,1,0:T(8,128)}) custom-call(f32[2,8,256,128]{3,2,1,0:T(8,128)} %get-tuple-element.4.final, f32[8,32,128]{2,1,0:T(8,128)} %get-tuple-element.5.gradient), custom_call_target="tpu_custom_call" | custom-call | tf_op jit(solution)/shard_map/pallas_call | solution.py:582
